TPU v7x, 32 devices: a whole 2x2x4 slice. The times are simulated.
32 devices in a mesh: groups: 2 (over y), rows: 4 (over z), sub: 2 (over x), rep: 2 (over core).
Axes of the slice: x: 2, y: 2, z: 4, core: 2. Of those that a mesh axis runs over, the one named last changes fastest.
Arguments:
- queries: float32 [256, 8192], P('rep', ('groups', 'rows', 'sub')), parts along dimension 1, may hold values from -10.5 to 10.5
- tiles: bfloat16 [128, 512, 512], P(('groups', 'rows', 'sub')), parts along dimension 0, may hold values from 0.01 to 10, as said below
- pair_blocks: int32 [128, 2], P('groups'), parts along dimension 0, may hold values from 0 to 7, as said below
Outputs:
- solution: float32 [256, 8192], P('rep', ('groups', 'rows', 'sub')), parts along dimension 1
- residual: float32 [256, 8192], P('rep', ('groups', 'rows', 'sub')), parts along dimension 1
There are 2 independent parts, one for each index of `groups`. A program takes and returns all parts, laid end to end along the dimension named above; each array names one. Nothing has to cross between parts.
Inputs may be any that keep to these rules, and one draw needn't show every extreme that they name: `pair_blocks`: row t describes tile t. Tiles 8 * b to 8 * b + 7 belong to block b, and the first of them is (b, b). Every tile of block b has a row block in the same set as b (same value of block // 2) and a column block no smaller than its row block, whose set lies less than 3 sets after b's. The tiles of one block name at most one column block in each later set. `tiles`: positive affinities.
All inputs are finite; a program needn't handle non-finite values.
Results may differ from a plain program's by a relative error of at most 0.01045.
Values may be sent and summed in bfloat16 or wider, within the bound.
A program may use at most 64 MiB of HBM per device.

v0:
```python
import functools

import jax
import jax.numpy as jnp
from jax import lax
from jax.experimental import pallas as pl
from jax.experimental.pallas import tpu as pltpu
from jax.sharding import PartitionSpec as P

SPAN = 3
ITERS = 3
DAMPING = 0.9
FAR = SPAN - 1
BASIS = ITERS + 1
CHUNKS = 2
MESH = pl.DeviceIdType.MESH
PAIRS = [(i, j) for i in range(BASIS) for j in range(i, BASIS)]


def plain(left, right):
    return jnp.dot(left, right, preferred_element_type=jnp.float32)


def turned(left, right):
    return lax.dot_general(
        left, right, (((1,), (1,)), ((), ())), preferred_element_type=jnp.float32
    )


def flag(condition):
    return jnp.where(condition, 1.0, 0.0).astype(jnp.float32)


def step_coefficients(gram):
    def inner(first, second):
        total = None
        for i in range(BASIS):
            for j in range(BASIS):
                if first[i] is None or second[j] is None:
                    continue
                term = first[i] * second[j] * gram[(min(i, j), max(i, j))]
                total = term if total is None else total + term
        return total

    def plus(first, factor, second):
        out = []
        for a, b in zip(first, second):
            if b is None:
                out.append(a)
            elif a is None:
                out.append(factor * b)
            else:
                out.append(a + factor * b)
        return out

    def mapped_of(vector):
        out = []
        for k in range(BASIS):
            low = vector[k - 1] if k else None
            if low is None:
                out.append(vector[k])
            elif vector[k] is None:
                out.append(-DAMPING * low)
            else:
                out.append(vector[k] - DAMPING * low)
        return out

    one = jnp.ones_like(gram[(0, 0)])
    found = [None] * BASIS
    residual = [one] + [None] * ITERS
    direction = list(residual)
    norm_now = gram[(0, 0)]
    for _ in range(ITERS):
        mapped = mapped_of(direction)
        step = norm_now / inner(direction, mapped)
        found = plus(found, step, direction)
        residual = plus(residual, -step, mapped)
        norm_next = inner(residual, residual)
        direction = plus(residual, norm_next / norm_now, direction)
        norm_now = norm_next
    return found, residual


def kernel(
    rows, sub, pairs, queries, tiles, found_out, residual_out,
    slots, panel, payload, fetched, back_out, back_in, acc, x_out, x_in, means, fields,
    deg_z, deg_z_in, deg_x, deg_x_in, row_sums, gram_all,
    panel_s, panel_r, pay_s, pay_r, back_s, back_r, x_s, x_r, mean_s, mean_r,
    dz_s, dz_r, dx_s, dx_r, gram_s, gram_r,
):
    r = lax.axis_index("rows")
    s = lax.axis_index("sub")
    count = rows * sub
    me = r * sub + s
    tile_count, order, _ = tiles.shape
    columns = queries.shape[0]
    own_slots = [(n, m) for n in range(sub) for m in range(n, sub)]
    slot_of = {pair: k for k, pair in enumerate(own_slots)}
    first_far = len(own_slots)

    def far_slot(n, off):
        return first_far + n * FAR + off - 1

    def device(row, column):
        return {"rows": row, "sub": column}

    for landing in (fetched, back_in, means, deg_z_in, deg_z, deg_x):
        landing[...] = jnp.zeros_like(landing)

    barrier = pltpu.get_barrier_semaphore()
    for j in range(1, count):
        peer = lax.rem(me + j, count)
        pl.semaphore_signal(
            barrier, inc=1, device_id=device(lax.div(peer, sub), lax.rem(peer, sub)), device_id_type=MESH
        )

    base = me * tile_count * 2
    tile_rows = [pairs[base + 2 * t] - r * sub for t in range(tile_count)]
    tile_cols = [pairs[base + 2 * t + 1] - r * sub for t in range(tile_count)]
    weights = []
    for n, m in own_slots:
        weights.append([flag((a == n) & (b == m)) for a, b in zip(tile_rows, tile_cols)])
    for n in range(sub):
        for off in range(1, SPAN):
            weights.append([
                flag((a == n) & (b >= off * sub) & (b < (off + 1) * sub))
                for a, b in zip(tile_rows, tile_cols)
            ])

    def named(off, column, block):
        peer = jnp.maximum((r - off) * sub + column, 0) * tile_count * 2
        hit = pairs[peer + 1] == block
        for t in range(1, tile_count):
            hit = hit | (pairs[peer + 2 * t + 1] == block)
        return flag(hit & (r >= off))

    wanted = [[named(off, s, r * sub + n) for n in range(sub)] for off in range(1, SPAN)]
    reads = []
    for off in range(1, SPAN):
        flags = []
        for m in range(sub):
            hit = tile_cols[0] == off * sub + m
            for t in range(1, tile_count):
                hit = hit | (tile_cols[t] == off * sub + m)
            flags.append(flag(hit))
        reads.append(flags)
    owned = [[named(off, column, me) for column in range(sub)] for off in range(1, SPAN)]

    chunk = 32

    @pl.loop(0, order // chunk)
    def _(i):
        span = pl.ds(pl.multiple_of(i * chunk, chunk), chunk)
        parts = [tiles[t, span, :].astype(jnp.float32) for t in range(tile_count)]
        for k, weight in enumerate(weights):
            total = weight[0] * parts[0]
            for t in range(1, tile_count):
                total = total + weight[t] * parts[t]
            slots[k, span, :] = total.astype(jnp.bfloat16)

    pl.semaphore_wait(barrier, count - 1)

    started = []

    def send(src, dst, send_sem, recv_sem, target, when=None):
        copy = pltpu.make_async_remote_copy(
            src_ref=src, dst_ref=dst, send_sem=send_sem, recv_sem=recv_sem,
            device_id=target, device_id_type=MESH,
        )
        started.append((copy, when))
        if when is None:
            copy.start()
        else:
            pl.when(when)(copy.start)
        return copy

    def arrive(copy, when=None):
        if when is None:
            copy.wait_recv()
        else:
            pl.when(when)(copy.wait_recv)

    ones = jnp.ones((16, order), jnp.bfloat16)
    for off in range(1, SPAN):
        for n in range(sub):
            deg_z[off - 1, n:n + 1, :] = plain(ones, slots[far_slot(n, off)])[:1]
    far_copies = {}
    for off in range(1, SPAN):
        for j in range(sub):
            target = device(jnp.minimum(r + off, rows - 1), lax.rem(s + j, sub))
            far_copies[off, j] = send(
                deg_z.at[off - 1], deg_z_in.at[off - 1, j],
                dz_s.at[off - 1, j], dz_r.at[off - 1, j], target, r + off < rows,
            )
    for n in range(sub):
        for m in range(sub):
            value = None
            if n <= m:
                value = turned(ones, slots[slot_of[(n, m)]])
            if m <= n:
                term = plain(ones, slots[slot_of[(m, n)]])
                value = term if value is None else value + term
            deg_x[n, m:m + 1, :] = value[:1]
        for off in range(1, SPAN):
            value = turned(ones, slots[far_slot(n, off)])[:1]
            for m in range(sub):
                k = off * sub + m
                deg_x[n, k:k + 1, :] = reads[off - 1][m] * value
    near_copies = []
    for j in range(1, sub):
        target = lax.rem(s + j, sub)
        near_copies.append(send(
            deg_x.at[target], deg_x_in.at[j - 1], dx_s.at[j - 1], dx_r.at[j - 1], device(r, target)
        ))
    total = deg_x[s]
    for j, copy in enumerate(near_copies):
        arrive(copy)
        total = total + deg_x_in[j]
    near_rows = total.shape[0]
    row_sums[...] = jnp.zeros_like(row_sums)
    row_sums[0:near_rows, :] = total
    for off in range(1, SPAN):
        first = near_rows + 8 * (off - 1)
        for j in range(sub):
            column = lax.rem(s - j + sub, sub)
            weight = owned[off - 1][0]
            for c in range(1, sub):
                weight = jnp.where(column == c, owned[off - 1][c], weight)
            arrive(far_copies[off, j], r >= off)
            row_sums[first:first + 8, :] = row_sums[first:first + 8, :] + weight * deg_z_in[off - 1, j]
    degree = jnp.sum(row_sums[...], axis=0, keepdims=True)
    root = 1.0 / jnp.sqrt(degree)

    def place_of(block):
        return lax.rem(s - block + sub, sub)

    def mean_row(distance, m):
        if distance >= 0:
            return distance * sub + m
        return near_rows + 8 * (-distance - 1) + m

    part = columns // CHUNKS
    spans = [slice(k * part, (k + 1) * part) for k in range(CHUNKS)]
    spread = (columns, 128)
    line = lax.broadcasted_iota(jnp.int32, (128, columns), 0)

    fields[0] = queries[...]
    for it in range(ITERS):
        scaled = root * fields[it]
        mean = jnp.mean(scaled, axis=1, keepdims=True).astype(jnp.bfloat16).astype(jnp.float32)
        panel[it, 0] = (scaled - mean).astype(jnp.bfloat16)
        gathers = {}
        for ch, span in enumerate(spans):
            for j in range(1, sub):
                gathers[ch, j] = send(
                    panel.at[it, 0, span], panel.at[it, j, span], panel_s.at[it, ch, j - 1],
                    panel_r.at[it, ch, j - 1], device(r, lax.rem(s + j, sub)),
                )
        means[it, FAR * sub] = jnp.broadcast_to(mean, spread).T[:16].astype(jnp.bfloat16)
        mean_copies = {}
        for d in range(-FAR, SPAN):
            for j in range(sub):
                k = (d + FAR) * sub + j
                if d == 0 and j == 0:
                    continue
                target = device(jnp.clip(r + d, 0, rows - 1), lax.rem(s + j, sub))
                mean_copies[d, j] = send(
                    means.at[it, FAR * sub], means.at[it, k], mean_s.at[it, k], mean_r.at[it, k],
                    target, None if d == 0 else (r + d >= 0) & (r + d < rows),
                )
        pays, backs = {}, {}
        for ch, span in enumerate(spans):
            for j in range(1, sub):
                arrive(gathers[ch, j])
            pieces = [panel[it, place_of(n), span] for n in range(sub)]
            for off in range(1, SPAN):
                total = wanted[off - 1][0] * pieces[0].astype(jnp.float32)
                for n in range(1, sub):
                    total = total + wanted[off - 1][n] * pieces[n].astype(jnp.float32)
                payload[it, off - 1, span] = total.astype(jnp.bfloat16)
                pays[ch, off] = send(
                    payload.at[it, off - 1, span], fetched.at[it, off - 1, span],
                    pay_s.at[it, ch, off - 1], pay_r.at[it, ch, off - 1],
                    device(jnp.maximum(r - off, 0), s), r >= off,
                )
            for off in range(1, SPAN):
                total = plain(pieces[0], slots[far_slot(0, off)])
                for n in range(1, sub):
                    total = total + plain(pieces[n], slots[far_slot(n, off)])
                back_out[it, off - 1, span] = total.astype(jnp.bfloat16)
                backs[ch, off] = send(
                    back_out.at[it, off - 1, span], back_in.at[it, off - 1, span],
                    back_s.at[it, ch, off - 1], back_r.at[it, ch, off - 1],
                    device(jnp.minimum(r + off, rows - 1), s), r + off < rows,
                )
        for n in range(sub):
            total = None
            for m in range(sub):
                source = panel[it, place_of(m)]
                if n <= m:
                    term = turned(source, slots[slot_of[(n, m)]])
                    total = term if total is None else total + term
                if m <= n:
                    term = plain(source, slots[slot_of[(m, n)]])
                    total = term if total is None else total + term
            acc[n] = total

        def finish(n, span):
            total = acc[n, span]
            for off in range(1, SPAN):
                weight = wanted[off - 1][0]
                for c in range(1, sub):
                    weight = jnp.where(n == c, wanted[off - 1][c], weight)
                total = total + weight * back_in[it, off - 1, span].astype(jnp.float32)
                total = total + turned(
                    fetched[it, off - 1, span], slots[far_slot(n, off)]
                )
            return total

        crossed = {}
        for ch, span in enumerate(spans):
            for off in range(1, SPAN):
                arrive(pays[ch, off], r + off < rows)
                arrive(backs[ch, off], r >= off)
            for j in range(1, sub):
                peer = lax.rem(s + j, sub)
                x_out[it, j - 1, span] = finish(peer, span).astype(jnp.bfloat16)
                crossed[ch, j] = send(
                    x_out.at[it, j - 1, span], x_in.at[it, j - 1, span], x_s.at[it, ch, j - 1],
                    x_r.at[it, ch, j - 1], device(r, peer),
                )
        for (d, j), copy in mean_copies.items():
            arrive(copy, None if d == 0 else (r - d >= 0) & (r - d < rows))
        table = jnp.zeros((128, columns), jnp.float32)
        for distance in range(-FAR, SPAN):
            for m in range(sub):
                row = means[it, (FAR - distance) * sub + place_of(m)].astype(jnp.float32)[:1]
                table = jnp.where(line == mean_row(distance, m), row, table)
        smooth = jnp.dot(
            table.T, row_sums[...], precision=lax.Precision.HIGHEST,
            preferred_element_type=jnp.float32,
        )
        for ch, span in enumerate(spans):
            total = smooth[span] + finish(s, span)
            for j in range(1, sub):
                arrive(crossed[ch, j])
                total = total + x_in[it, j - 1, span].astype(jnp.float32)
            fields[it + 1, span] = root * total

    lane = lax.broadcasted_iota(jnp.int32, (columns, 128), 1)
    table = jnp.zeros((columns, 128), jnp.float32)
    for k, (i, j) in enumerate(PAIRS):
        table = jnp.where(lane == k, jnp.sum(fields[i] * fields[j], axis=1, keepdims=True), table)
    gram_all[0] = table.T[:16]
    gram_copies = []
    for j in range(1, count):
        peer = lax.rem(me + j, count)
        gram_copies.append(send(
            gram_all.at[0], gram_all.at[j], gram_s.at[j - 1], gram_r.at[j - 1],
            device(lax.div(peer, sub), lax.rem(peer, sub)),
        ))
    total = gram_all[0]
    for j, copy in enumerate(gram_copies, 1):
        arrive(copy)
        total = total + gram_all[j]
    gram = {pair: total[k:k + 1] for k, pair in enumerate(PAIRS)}
    found, residual = step_coefficients(gram)
    rows_of = [c for c in found if c is not None] + residual
    table = jnp.zeros((128, columns), jnp.float32)
    for k, row in enumerate(rows_of):
        table = jnp.where(line == k, row, table)
    table = table.T
    total = table[:, 0:1] * fields[0]
    for k in range(1, ITERS):
        total = total + table[:, k:k + 1] * fields[k]
    found_out[...] = total
    total = table[:, ITERS:ITERS + 1] * fields[0]
    for k in range(1, BASIS):
        total = total + table[:, ITERS + k:ITERS + k + 1] * fields[k]
    residual_out[...] = total
    for copy, when in started:
        if when is None:
            copy.wait_send()
        else:
            pl.when(when)(copy.wait_send)


def local(queries, tiles, pair_blocks):
    rows = lax.axis_size("rows")
    sub = lax.axis_size("sub")
    count = rows * sub
    columns, order = queries.shape
    slot_count = sub * (sub + 1) // 2 + sub * FAR
    near_rows = -(-SPAN * sub // 8) * 8
    wide = lambda *shape: pltpu.VMEM(shape, jnp.float32)
    narrow = lambda *shape: pltpu.VMEM(shape, jnp.bfloat16)
    dma = lambda *shape: pltpu.SemaphoreType.DMA(shape)
    both = lambda *shape: [dma(*shape), dma(*shape)]
    vmem = pl.BlockSpec(memory_space=pltpu.VMEM)
    out = jax.ShapeDtypeStruct((columns, order), jnp.float32)
    return pl.pallas_call(
        functools.partial(kernel, rows, sub),
        out_shape=(out, out),
        in_specs=[pl.BlockSpec(memory_space=pltpu.SMEM), vmem, vmem],
        out_specs=(vmem, vmem),
        scratch_shapes=[
            narrow(slot_count, order, order),
            narrow(ITERS, sub, columns, order),
            narrow(ITERS, FAR, columns, order),
            narrow(ITERS, FAR, columns, order),
            narrow(ITERS, FAR, columns, order),
            narrow(ITERS, FAR, columns, order),
            wide(sub, columns, order),
            narrow(ITERS, sub - 1, columns, order),
            narrow(ITERS, sub - 1, columns, order),
            narrow(ITERS, (FAR + SPAN) * sub, 16, columns),
            wide(BASIS, columns, order),
            wide(FAR, 8, order),
            wide(FAR, sub, 8, order),
            wide(sub, near_rows, order),
            wide(sub - 1, near_rows, order),
            wide(128, order),
            wide(count, 16, columns),
            *both(ITERS, CHUNKS, sub - 1),
            *both(ITERS, CHUNKS, FAR),
            *both(ITERS, CHUNKS, FAR),
            *both(ITERS, CHUNKS, sub - 1),
            *both(ITERS, (FAR + SPAN) * sub),
            *both(FAR, sub),
            *both(sub - 1),
            *both(count - 1),
        ],
        compiler_params=pltpu.CompilerParams(
            collective_id=0, has_side_effects=True, vmem_limit_bytes=48 * 1024 * 1024
        ),
    )(pair_blocks.reshape(-1), queries, tiles)


def solution(mesh):
    return jax.shard_map(
        local,
        mesh=mesh,
        in_specs=(
            P("rep", ("groups", "rows", "sub")),
            P(("groups", "rows", "sub"), None, None),
            P("groups", None),
        ),
        out_specs=(P("rep", ("groups", "rows", "sub")), P("rep", ("groups", "rows", "sub"))),
        check_vma=False,
    )
```

profile of v0, /device:TPU:0, one launch (start us, length us, event | category | flops | bytes accessed | tf_op | source)
XLA Modules:
  0.0 70.2 jit_solution(15412653654004400280)
XLA Ops:
  0.6 0.8 %copy.6 = s32[64,2]{1,0:T(8,128)S(1)} copy(s32[64,2]{0,1:T(2,128)} %param.5) | data formatting | bytes 1024 | tf_op args[2]
  1.4 0.1 reshape.7.pairs
  1.5 0.0 copy-start
  1.5 2.2 %copy-done = bf16[8,512,512]{2,1,0:T(8,128)(2,1)S(1)} copy-done((bf16[8,512,512]{2,1,0:T(8,128)(2,1)S(1)}, bf16[8,512,512]{2,1,0:T(8,128)(2,1)}, u32[]{:S(2)}) %copy-start) | copy-done | bytes 4194328
  3.7 0.0 copy-start.1
  3.7 0.9 %copy-done.1 = f32[128,512]{1,0:T(8,128)S(1)} copy-done((f32[128,512]{1,0:T(8,128)S(1)}, f32[128,512]{1,0:T(8,128)}, u32[]{:S(2)}) %copy-start.1) | copy-done | bytes 262168
  4.7 64.1 %shard_map.50 = (f32[128,512]{1,0:T(8,128)S(1)}, f32[128,512]{1,0:T(8,128)S(1)}) custom-call(s32[128]{0:T(128)S(1)} %reshape.7.pairs, f32[128,512]{1,0:T(8,128)S(1)} %copy-done.1, bf16[8,512,512]{2,1,0:T(8,128)(2,1)S(1)} %copy-done), custom_call_target="tpu_custom_call" | custom-call | tf_op jit(solution)/shard_map/pallas_call | solution.py:401
  68.8 0.7 %copy.9 = f32[128,512]{1,0:T(8,128)} copy(f32[128,512]{1,0:T(8,128)S(1)} %get-tuple-element.4) | data formatting | bytes 524288
  69.5 0.7 %copy.10 = f32[128,512]{1,0:T(8,128)} copy(f32[128,512]{1,0:T(8,128)S(1)} %get-tuple-element.5) | data formatting | bytes 524288
Async XLA Ops:
  1.5 2.2 %copy-start = (bf16[8,512,512]{2,1,0:T(8,128)(2,1)S(1)}, bf16[8,512,512]{2,1,0:T(8,128)(2,1)}, u32[]{:S(2)}) copy-start(bf16[8,512,512]{2,1,0:T(8,128)(2,1)} %tiles.1) | copy-start | bytes 12582916
  3.7 0.9 %copy-start.1 = (f32[128,512]{1,0:T(8,128)S(1)}, f32[128,512]{1,0:T(8,128)}, u32[]{:S(2)}) copy-start(f32[128,512]{1,0:T(8,128)} %queries.1) | copy-start | bytes 786436
where the time goes:
time: 70.4 us; the launch traced here: 70.2 us
  Pallas kernels  64.1 us (91%)
  local copies, waits for them, and re-layouts  5.45 us (8%)
    pallas_call x1, Pallas kernels, local(): pl.pallas_call(functools.partial(kernel, rows, sub), out_shape=(out, out)...  64.1 us
    unnamed x7, local copies, waits for them, and re-layouts  5.31 us

commit v1 on v0

--- a/solution.py
+++ b/solution.py
@@ -12,7 +12,8 @@
 DAMPING = 0.9
 FAR = SPAN - 1
 BASIS = ITERS + 1
-CHUNKS = 2
+CHUNKS = 4
+GROUPS = 4
 MESH = pl.DeviceIdType.MESH
 PAIRS = [(i, j) for i in range(BASIS) for j in range(i, BASIS)]
 
@@ -82,8 +83,8 @@
 
 
 def kernel(
-    rows, sub, pairs, queries, tiles, found_out, residual_out,
-    slots, panel, payload, fetched, back_out, back_in, acc, x_out, x_in, means, fields,
+    rows, sub, pairs, queries, tiles_far, found_out, residual_out,
+    tiles, load_s, slots, panel, payload, fetched, back_out, back_in, acc, x_out, x_in, means, fields,
     deg_z, deg_z_in, deg_x, deg_x_in, row_sums, gram_all,
     panel_s, panel_r, pay_s, pay_r, back_s, back_r, x_s, x_r, mean_s, mean_r,
     dz_s, dz_r, dx_s, dx_r, gram_s, gram_r,
@@ -104,6 +105,13 @@
     def device(row, column):
         return {"rows": row, "sub": column}
 
+    group = order // GROUPS
+    loads = []
+    for g in range(GROUPS):
+        span = pl.ds(g * group, group)
+        loads.append(pltpu.make_async_copy(tiles_far.at[:, span], tiles.at[:, span], load_s.at[g]))
+        loads[-1].start()
+
     for landing in (fetched, back_in, means, deg_z_in, deg_z, deg_x):
         landing[...] = jnp.zeros_like(landing)
 
@@ -148,8 +156,7 @@
 
     chunk = 32
 
-    @pl.loop(0, order // chunk)
-    def _(i):
+    def sum_tiles(i):
         span = pl.ds(pl.multiple_of(i * chunk, chunk), chunk)
         parts = [tiles[t, span, :].astype(jnp.float32) for t in range(tile_count)]
         for k, weight in enumerate(weights):
@@ -157,6 +164,10 @@
             for t in range(1, tile_count):
                 total = total + weight[t] * parts[t]
             slots[k, span, :] = total.astype(jnp.bfloat16)
+
+    for g in range(GROUPS):
+        loads[g].wait()
+        pl.loop(g * group // chunk, (g + 1) * group // chunk)(sum_tiles)
 
     pl.semaphore_wait(barrier, count - 1)
 
@@ -273,7 +284,7 @@
             for j in range(1, sub):
                 arrive(gathers[ch, j])
             pieces = [panel[it, place_of(n), span] for n in range(sub)]
-            for off in range(1, SPAN):
+            for off in range(FAR, 0, -1):
                 total = wanted[off - 1][0] * pieces[0].astype(jnp.float32)
                 for n in range(1, sub):
                     total = total + wanted[off - 1][n] * pieces[n].astype(jnp.float32)
@@ -283,7 +294,7 @@
                     pay_s.at[it, ch, off - 1], pay_r.at[it, ch, off - 1],
                     device(jnp.maximum(r - off, 0), s), r >= off,
                 )
-            for off in range(1, SPAN):
+            for off in range(FAR, 0, -1):
                 total = plain(pieces[0], slots[far_slot(0, off)])
                 for n in range(1, sub):
                     total = total + plain(pieces[n], slots[far_slot(n, off)])
@@ -401,9 +412,11 @@
     return pl.pallas_call(
         functools.partial(kernel, rows, sub),
         out_shape=(out, out),
-        in_specs=[pl.BlockSpec(memory_space=pltpu.SMEM), vmem, vmem],
+        in_specs=[pl.BlockSpec(memory_space=pltpu.SMEM), vmem, pl.BlockSpec(memory_space=pl.ANY)],
         out_specs=(vmem, vmem),
         scratch_shapes=[
+            narrow(*tiles.shape),
+            dma(GROUPS),
             narrow(slot_count, order, order),
             narrow(ITERS, sub, columns, order),
             narrow(ITERS, FAR, columns, order),

time: 70.4 us -> 69.7 us (0.990)
    pallas_call x1, Pallas kernels: 64.1 us -> 63.4 us  [local(): pl.pallas_call(functools.partial(kernel, rows, sub), out_shape=(out, out)...]
where the time goes in v1:
time: 69.7 us; the launch traced here: 69.5 us
  Pallas kernels  63.4 us (91%)
  local copies, waits for them, and re-layouts  5.45 us (8%)
    pallas_call x1, Pallas kernels, local(): pl.pallas_call(functools.partial(kernel, rows, sub), out_shape=(out, out)...  63.4 us
    unnamed x7, local copies, waits for them, and re-layouts  5.31 us

profile of v1, /device:TPU:0, one launch (start us, length us, event | category | flops | bytes accessed | tf_op | source)
XLA Modules:
  0.0 69.5 jit_solution(10169185375486609029)
XLA Ops:
  0.6 0.8 %copy.6 = s32[64,2]{1,0:T(8,128)S(1)} copy(s32[64,2]{0,1:T(2,128)} %param.5) | data formatting | bytes 1024 | tf_op args[2]
  1.4 0.1 reshape.7.pairs
  1.5 0.0 copy-start
  1.5 2.2 %copy-done = bf16[8,512,512]{2,1,0:T(8,128)(2,1)S(1)} copy-done((bf16[8,512,512]{2,1,0:T(8,128)(2,1)S(1)}, bf16[8,512,512]{2,1,0:T(8,128)(2,1)}, u32[]{:S(2)}) %copy-start) | copy-done | bytes 4194328
  3.7 0.0 copy-start.1
  3.7 0.9 %copy-done.1 = f32[128,512]{1,0:T(8,128)S(1)} copy-done((f32[128,512]{1,0:T(8,128)S(1)}, f32[128,512]{1,0:T(8,128)}, u32[]{:S(2)}) %copy-start.1) | copy-done | bytes 262168
  4.7 63.4 %shard_map.50 = (f32[128,512]{1,0:T(8,128)S(1)}, f32[128,512]{1,0:T(8,128)S(1)}) custom-call(s32[128]{0:T(128)S(1)} %reshape.7.pairs, f32[128,512]{1,0:T(8,128)S(1)} %copy-done.1, bf16[8,512,512]{2,1,0:T(8,128)(2,1)S(1)} %copy-done), custom_call_target="tpu_custom_call" | custom-call | tf_op jit(solution)/shard_map/pallas_call | solution.py:412
  68.0 0.7 %copy.9 = f32[128,512]{1,0:T(8,128)} copy(f32[128,512]{1,0:T(8,128)S(1)} %get-tuple-element.4) | data formatting | bytes 524288
  68.8 0.7 %copy.10 = f32[128,512]{1,0:T(8,128)} copy(f32[128,512]{1,0:T(8,128)S(1)} %get-tuple-element.5) | data formatting | bytes 524288
Async XLA Ops:
  1.5 2.2 %copy-start = (bf16[8,512,512]{2,1,0:T(8,128)(2,1)S(1)}, bf16[8,512,512]{2,1,0:T(8,128)(2,1)}, u32[]{:S(2)}) copy-start(bf16[8,512,512]{2,1,0:T(8,128)(2,1)} %tiles_far.1) | copy-start | bytes 12582916
  3.7 0.9 %copy-start.1 = (f32[128,512]{1,0:T(8,128)S(1)}, f32[128,512]{1,0:T(8,128)}, u32[]{:S(2)}) copy-start(f32[128,512]{1,0:T(8,128)} %queries.1) | copy-start | bytes 786436

commit v2 on v0

--- a/solution.py
+++ b/solution.py
@@ -12,7 +12,8 @@
 DAMPING = 0.9
 FAR = SPAN - 1
 BASIS = ITERS + 1
-CHUNKS = 2
+CHUNKS = 4
+GROUPS = 4
 MESH = pl.DeviceIdType.MESH
 PAIRS = [(i, j) for i in range(BASIS) for j in range(i, BASIS)]
 
@@ -82,8 +83,8 @@
 
 
 def kernel(
-    rows, sub, pairs, queries, tiles, found_out, residual_out,
-    slots, panel, payload, fetched, back_out, back_in, acc, x_out, x_in, means, fields,
+    rows, sub, pairs, queries, tiles_far, found_out, residual_out,
+    tiles, load_s, slots, panel, payload, fetched, back_out, back_in, acc, x_out, x_in, means, fields,
     deg_z, deg_z_in, deg_x, deg_x_in, row_sums, gram_all,
     panel_s, panel_r, pay_s, pay_r, back_s, back_r, x_s, x_r, mean_s, mean_r,
     dz_s, dz_r, dx_s, dx_r, gram_s, gram_r,
@@ -104,6 +105,13 @@
     def device(row, column):
         return {"rows": row, "sub": column}
 
+    group = order // GROUPS
+    loads = []
+    for g in range(GROUPS):
+        span = pl.ds(g * group, group)
+        loads.append(pltpu.make_async_copy(tiles_far.at[:, span], tiles.at[:, span], load_s.at[g]))
+        loads[-1].start()
+
     for landing in (fetched, back_in, means, deg_z_in, deg_z, deg_x):
         landing[...] = jnp.zeros_like(landing)
 
@@ -148,8 +156,7 @@
 
     chunk = 32
 
-    @pl.loop(0, order // chunk)
-    def _(i):
+    def sum_tiles(i):
         span = pl.ds(pl.multiple_of(i * chunk, chunk), chunk)
         parts = [tiles[t, span, :].astype(jnp.float32) for t in range(tile_count)]
         for k, weight in enumerate(weights):
@@ -157,6 +164,10 @@
             for t in range(1, tile_count):
                 total = total + weight[t] * parts[t]
             slots[k, span, :] = total.astype(jnp.bfloat16)
+
+    for g in range(GROUPS):
+        loads[g].wait()
+        pl.loop(g * group // chunk, (g + 1) * group // chunk)(sum_tiles)
 
     pl.semaphore_wait(barrier, count - 1)
 
@@ -257,17 +268,6 @@
                     panel_r.at[it, ch, j - 1], device(r, lax.rem(s + j, sub)),
                 )
         means[it, FAR * sub] = jnp.broadcast_to(mean, spread).T[:16].astype(jnp.bfloat16)
-        mean_copies = {}
-        for d in range(-FAR, SPAN):
-            for j in range(sub):
-                k = (d + FAR) * sub + j
-                if d == 0 and j == 0:
-                    continue
-                target = device(jnp.clip(r + d, 0, rows - 1), lax.rem(s + j, sub))
-                mean_copies[d, j] = send(
-                    means.at[it, FAR * sub], means.at[it, k], mean_s.at[it, k], mean_r.at[it, k],
-                    target, None if d == 0 else (r + d >= 0) & (r + d < rows),
-                )
         pays, backs = {}, {}
         for ch, span in enumerate(spans):
             for j in range(1, sub):
@@ -292,6 +292,17 @@
                     back_out.at[it, off - 1, span], back_in.at[it, off - 1, span],
                     back_s.at[it, ch, off - 1], back_r.at[it, ch, off - 1],
                     device(jnp.minimum(r + off, rows - 1), s), r + off < rows,
+                )
+        mean_copies = {}
+        for d in range(-FAR, SPAN):
+            for j in range(sub):
+                k = (d + FAR) * sub + j
+                if d == 0 and j == 0:
+                    continue
+                target = device(jnp.clip(r + d, 0, rows - 1), lax.rem(s + j, sub))
+                mean_copies[d, j] = send(
+                    means.at[it, FAR * sub], means.at[it, k], mean_s.at[it, k], mean_r.at[it, k],
+                    target, None if d == 0 else (r + d >= 0) & (r + d < rows),
                 )
         for n in range(sub):
             total = None
@@ -401,9 +412,11 @@
     return pl.pallas_call(
         functools.partial(kernel, rows, sub),
         out_shape=(out, out),
-        in_specs=[pl.BlockSpec(memory_space=pltpu.SMEM), vmem, vmem],
+        in_specs=[pl.BlockSpec(memory_space=pltpu.SMEM), vmem, pl.BlockSpec(memory_space=pl.ANY)],
         out_specs=(vmem, vmem),
         scratch_shapes=[
+            narrow(*tiles.shape),
+            dma(GROUPS),
             narrow(slot_count, order, order),
             narrow(ITERS, sub, columns, order),
             narrow(ITERS, FAR, columns, order),

time: 70.4 us -> 69.6 us (0.989)
  Pallas kernels: 64.1 us -> 63.3 us
    pallas_call x1, Pallas kernels: 64.1 us -> 63.3 us  [local(): pl.pallas_call(functools.partial(kernel, rows, sub), out_shape=(out, out)...]
where the time goes in v2:
time: 69.6 us; the launch traced here: 69.4 us
  Pallas kernels  63.3 us (91%)
  local copies, waits for them, and re-layouts  5.45 us (8%)
    pallas_call x1, Pallas kernels, local(): pl.pallas_call(functools.partial(kernel, rows, sub), out_shape=(out, out)...  63.3 us
    unnamed x7, local copies, waits for them, and re-layouts  5.31 us

profile of v2, /device:TPU:0, one launch (start us, length us, event | category | flops | bytes accessed | tf_op | source)
XLA Modules:
  0.0 69.4 jit_solution(14101600334904221966)
XLA Ops:
  0.6 0.8 %copy.6 = s32[64,2]{1,0:T(8,128)S(1)} copy(s32[64,2]{0,1:T(2,128)} %param.5) | data formatting | bytes 1024 | tf_op args[2]
  1.4 0.1 reshape.7.pairs
  1.5 0.0 copy-start
  1.5 2.2 %copy-done = bf16[8,512,512]{2,1,0:T(8,128)(2,1)S(1)} copy-done((bf16[8,512,512]{2,1,0:T(8,128)(2,1)S(1)}, bf16[8,512,512]{2,1,0:T(8,128)(2,1)}, u32[]{:S(2)}) %copy-start) | copy-done | bytes 4194328
  3.7 0.0 copy-start.1
  3.7 0.9 %copy-done.1 = f32[128,512]{1,0:T(8,128)S(1)} copy-done((f32[128,512]{1,0:T(8,128)S(1)}, f32[128,512]{1,0:T(8,128)}, u32[]{:S(2)}) %copy-start.1) | copy-done | bytes 262168
  4.7 63.3 %shard_map.50 = (f32[128,512]{1,0:T(8,128)S(1)}, f32[128,512]{1,0:T(8,128)S(1)}) custom-call(s32[128]{0:T(128)S(1)} %reshape.7.pairs, f32[128,512]{1,0:T(8,128)S(1)} %copy-done.1, bf16[8,512,512]{2,1,0:T(8,128)(2,1)S(1)} %copy-done), custom_call_target="tpu_custom_call" | custom-call | tf_op jit(solution)/shard_map/pallas_call | solution.py:412
  68.0 0.7 %copy.9 = f32[128,512]{1,0:T(8,128)} copy(f32[128,512]{1,0:T(8,128)S(1)} %get-tuple-element.4) | data formatting | bytes 524288
  68.7 0.7 %copy.10 = f32[128,512]{1,0:T(8,128)} copy(f32[128,512]{1,0:T(8,128)S(1)} %get-tuple-element.5) | data formatting | bytes 524288
Async XLA Ops:
  1.5 2.2 %copy-start = (bf16[8,512,512]{2,1,0:T(8,128)(2,1)S(1)}, bf16[8,512,512]{2,1,0:T(8,128)(2,1)}, u32[]{:S(2)}) copy-start(bf16[8,512,512]{2,1,0:T(8,128)(2,1)} %tiles_far.1) | copy-start | bytes 12582916
  3.7 0.9 %copy-start.1 = (f32[128,512]{1,0:T(8,128)S(1)}, f32[128,512]{1,0:T(8,128)}, u32[]{:S(2)}) copy-start(f32[128,512]{1,0:T(8,128)} %queries.1) | copy-start | bytes 786436
